TPU v7x, 32 devices: a whole 2x2x4 slice. The times are simulated.
32 devices in a mesh: groups: 2 (over x), seq: 16 (over z, y, core).
Axes of the slice: x: 2, y: 2, z: 4, core: 2. Of those that a mesh axis runs over, the one named last changes fastest.
Arguments:
- tokens: bfloat16 [32768, 2048], P(('groups', 'seq')), parts along dimension 0, may hold values from -64 to 64, as said below
- gain_mix: float32 [2048], replicated, may hold values from 0.1 to 1.9
- gain_mlp: float32 [2048], replicated, may hold values from 0.1 to 1.9
- block_mix: bfloat16 [1024, 1024], replicated, may hold values from -0.1875 to 0.1875
- cross_mix: bfloat16 [16, 16], replicated, may hold values from -1.5 to 1.5
- w_in: bfloat16 [2048, 1024], P('seq'), may hold values from -0.25 to 0.25
- w_out: bfloat16 [4096, 512], P('seq'), may hold values from -0.1875 to 0.1875
Outputs:
- mixed: bfloat16 [32768, 2048], P(('groups', 'seq')), parts along dimension 0
There are 2 independent parts, one for each index of `groups`. A program takes and returns all parts, laid end to end along the dimension named above; an argument that names none is the same for every part. Nothing has to cross between parts.
Inputs may be any that keep to these rules, and one draw needn't show every extreme that they name: `tokens`: activations with independent scales per channel and per position.
All inputs are finite; a program needn't handle non-finite values.
Results may differ from a plain program's by a relative error of at most 0.0085.
Values may be sent and summed in bfloat16 or wider, within the bound.
A program may use at most 128 MiB of HBM per device.

v0:
```python
import jax
import jax.numpy as jnp
from jax import lax
from jax.sharding import PartitionSpec as P

NCB = 4
BLK = 1024


def rms_scale(values, gain):
    mean_square = jnp.mean(values * values, axis=-1, keepdims=True)
    return values * lax.rsqrt(mean_square + 1e-06) * gain


def shards(tokens, gain_mix, gain_mlp, block_mix, cross_mix, w_in, w_out):
    rows, width = tokens.shape
    nblocks = rows // BLK
    raw = tokens.astype(jnp.float32)
    normed = rms_scale(raw, gain_mix).astype(jnp.bfloat16)
    within = jnp.einsum(
        "hp,ops->ohs",
        block_mix,
        normed.reshape(nblocks, BLK, width),
        preferred_element_type=jnp.float32,
    ).astype(jnp.bfloat16)
    mixed_cols = jnp.einsum(
        "ai,ijd->ajd",
        cross_mix,
        lax.all_to_all(within, "seq", split_axis=1, concat_axis=0, tiled=True),
        preferred_element_type=jnp.float32,
    ).astype(jnp.bfloat16)
    across = lax.all_to_all(mixed_cols, "seq", split_axis=0, concat_axis=1, tiled=True)
    gated = (
        raw + normed.astype(jnp.float32) * across.reshape(rows, width).astype(jnp.float32)
    ).astype(jnp.bfloat16)
    inner = rms_scale(gated.astype(jnp.float32), gain_mlp).astype(jnp.bfloat16)
    weight_in = lax.all_gather(w_in, "seq", axis=0, tiled=True)
    hidden = jnp.einsum(
        "rcd,cdf->rcf",
        inner.reshape(rows, NCB, width // NCB),
        weight_in.reshape(NCB, width // NCB, -1),
        preferred_element_type=jnp.float32,
    )
    hidden = jax.nn.gelu(hidden).astype(jnp.bfloat16)
    weight_out = lax.all_gather(w_out, "seq", axis=0, tiled=True)
    output = jnp.einsum(
        "rcf,cfd->rcd",
        hidden,
        weight_out.reshape(NCB, hidden.shape[2], -1),
        preferred_element_type=jnp.float32,
    )
    return (gated.astype(jnp.float32) + output.reshape(rows, width)).astype(jnp.bfloat16)


def solution(mesh):
    in_specs = (P(("groups", "seq"), None), P(), P(), P(), P(), P("seq", None), P("seq", None))
    out_specs = P(("groups", "seq"), None)
    return jax.shard_map(shards, mesh=mesh, in_specs=in_specs, out_specs=out_specs, check_vma=False)
```

profile of v0, /device:TPU:13, one launch (start us, length us, event | category | flops | bytes accessed | tf_op | source)
XLA Modules:
  0.0 401.5 jit_solution(3762509726161138529)
XLA Ops:
  6.5 3.2 fusion.8
  9.8 9.2 %convert_bitcast_fusion.1 = bf16[1,1024,2048]{1,2,0:T(8,128)(2,1)} fusion(bf16[1024,1024]{1,0:T(8,128)(2,1)S(1)} %copy-done, bf16[1024,2048]{1,0:T(8,128)(2,1)} %param.7, f32[2048]{0:T(1024)} %param.8, f32[1024]{0:T(1024)S(1)} %add_rsqrt_fusion.1), kind=kOutput, calls=%fused_computation.29 | convolution fusion | flops 4305453056 | bytes 10498048 | tf_op jit(solution)/shard_map/hp,ops->ohs/dot_general | solution.py:20
  19.0 20.6 %copy.17 = bf16[1,1024,2048]{2,0,1:T(2,128)(2,1)} copy(bf16[1,1024,2048]{1,2,0:T(8,128)(2,1)} %convert_bitcast_fusion.1) | data formatting | bytes 8388608 | tf_op jit(solution)/shard_map/convert_element_type | solution.py:25
  39.6 0.5 broadcast.36
  40.2 26.7 %reduce = bf16[1024,2048]{1,0:T(8,128)(2,1)} reduce(bf16[1024,1,2048]{2,1,0:T(2,128)(2,1)} %bitcast.34, bf16[]{:T(256)} %broadcast.36), dimensions={1}, to_apply=%bitcast.28.reduce_sub_computation | reduce | bytes 8388610
  66.9 11.4 %reshape.51 = bf16[16,2,65536]{2,1,0:T(2,128)(2,1)} reshape(bf16[1024,2048]{1,0:T(8,128)(2,1)} %reduce) | data formatting | bytes 8388608
  78.3 6.6 %all-to-all-start = ((bf16[16,2,65536]{2,1,0:T(2,128)(2,1)}), bf16[16,2,65536]{2,1,0:T(2,128)(2,1)}, u32[]{:S(2)}, u32[]{:S(2)}) async-start(bf16[16,2,65536]{2,1,0:T(2,128)(2,1)} %reshape.51), calls=%async_computation | async-start | bytes 8388608 | tf_op jit(solution)/shard_map/all_to_all | solution.py:29
  84.8 0.2 all-gather.3.cloned.1.call-start
  85.0 0.5 all-gather.3.cloned.1.call-update
  85.5 117.0 %all-to-all-done = bf16[16,2,65536]{2,1,0:T(2,128)(2,1)} async-done(((bf16[16,2,65536]{2,1,0:T(2,128)(2,1)}), bf16[16,2,65536]{2,1,0:T(2,128)(2,1)}, u32[]{:S(2)}, u32[]{:S(2)}) %all-to-all-start) | async-done | bytes 4194336 | tf_op jit(solution)/shard_map/all_to_all | solution.py:29
  202.6 12.4 %reshape.52 = bf16[1024,1,2048]{2,1,0:T(2,128)(2,1)} reshape(bf16[16,2,65536]{2,1,0:T(2,128)(2,1)} %all-to-all-done) | data formatting | bytes 8388608
  214.9 6.0 %copy.24 = bf16[1,1024,2048]{2,1,0:T(8,128)(2,1)S(1)} copy(bf16[1,1024,2048]{2,0,1:T(2,128)(2,1)} %bitcast.35) | data formatting | bytes 8388608
  221.0 4.8 %convert_bitcast_fusion = bf16[16,64,2048]{2,0,1:T(8,128)(2,1)S(1)} fusion(bf16[16,64,2048]{2,1,0:T(8,128)(2,1)S(1)} %bitcast.36, bf16[16,16]{1,0:T(8,128)(2,1)S(1)} %copy-done.5), kind=kOutput, calls=%fused_computation.28 | convolution fusion | flops 69206016 | bytes 8389120 | tf_op jit(solution)/shard_map/ai,ijd->ajd/dot_general | solution.py:26
  225.8 4.3 %copy.19 = bf16[16,64,2048]{2,1,0:T(8,128)(2,1)} copy(bf16[16,64,2048]{2,0,1:T(8,128)(2,1)S(1)} %convert_bitcast_fusion) | data formatting | bytes 8388608 | tf_op jit(solution)/shard_map/convert_element_type | solution.py:31
  230.1 4.9 %all-to-all-start.1 = ((bf16[16,64,2048]{2,1,0:T(8,128)(2,1)}), bf16[16,64,2048]{2,1,0:T(8,128)(2,1)}, u32[]{:S(2)}, u32[]{:S(2)}) async-start(bf16[16,64,2048]{2,1,0:T(8,128)(2,1)} %copy.19), calls=%async_computation.1 | async-start | bytes 8388608 | tf_op jit(solution)/shard_map/all_to_all | solution.py:32
  235.0 0.3 all-gather.5.cloned.1.call-start
  235.3 0.5 all-gather.5.cloned.1.call-update
  235.8 117.0 %all-to-all-done.1 = bf16[16,64,2048]{2,1,0:T(8,128)(2,1)} async-done(((bf16[16,64,2048]{2,1,0:T(8,128)(2,1)}), bf16[16,64,2048]{2,1,0:T(8,128)(2,1)}, u32[]{:S(2)}, u32[]{:S(2)}) %all-to-all-start.1) | async-done | bytes 4194336 | tf_op jit(solution)/shard_map/all_to_all | solution.py:32
  352.8 5.0 %fusion.12 = (f32[1024]{0:T(1024)S(1)}, bf16[1024,2048]{1,0:T(8,128)(2,1)S(1)}) fusion(bf16[16,64,2048]{2,1,0:T(8,128)(2,1)} %all-to-all-done.1, f32[2048]{0:T(1024)S(1)} %copy-done.3, f32[1024]{0:T(1024)S(1)} %add_rsqrt_fusion.1, bf16[1024,2048]{1,0:T(8,128)(2,1)} %param.7), kind=kLoop, calls=%fused_computation.19 | loop fusion | flops 25164800 | bytes 12599296 | tf_op jit(solution)/shard_map/reduce_sum | solution.py:11
  357.8 1.9 copy-done.2
  359.7 3.0 fusion.14
  362.7 14.3 %fusion.28 = f32[4,1024,512]{1,2,0:T(8,128)} fusion(bf16[4,1024,512]{2,1,0:T(8,128)(2,1)} %bitcast.40, bf16[4,512,1024]{2,1,0:T(8,128)(2,1)} %bitcast.39, bf16[128,4,8,512]{3,2,1,0:T(8,128)(2,1)} %bitcast.38), kind=kOutput, calls=%fused_computation.32 | convolution fusion | flops 8627683328 | bytes 20971520 | tf_op jit(solution)/shard_map/rcf,cfd->rcd/dot_general | solution.py:46
  377.1 9.3 %copy.22 = f32[1024,2048]{1,0:T(8,128)} copy(f32[1024,2048]{0,1:T(8,128)} %bitcast.37) | data formatting | bytes 16777216 | tf_op jit(solution)/shard_map/reshape | solution.py:52
  386.4 8.3 %fusion.15 = bf16[1024,2048]{1,0:T(8,128)(2,1)} fusion(f32[1024,2048]{1,0:T(8,128)} %copy.22, bf16[1024,2048]{1,0:T(8,128)(2,1)} %copy-done.2), kind=kLoop, calls=%fused_computation.22 | loop fusion | flops 6291456 | bytes 16777216 | tf_op jit(solution)/shard_map/convert_element_type | solution.py:52
  (15 shorter events, 0.0 us)
Async XLA Ops:
  6.5 3.2 copy-start
  78.3 124.3 %all-to-all-start = ((bf16[16,2,65536]{2,1,0:T(2,128)(2,1)}), bf16[16,2,65536]{2,1,0:T(2,128)(2,1)}, u32[]{:S(2)}, u32[]{:S(2)}) async-start(bf16[16,2,65536]{2,1,0:T(2,128)(2,1)} %reshape.51), calls=%async_computation | async-start | bytes 8388608 | tf_op jit(solution)/shard_map/all_to_all | solution.py:29
  84.8 277.9 %all-gather.3.cloned.1.call-start = ((), (), s32[]{:S(2)}) async-start(), calls=%async_computation.2 | async-start | bytes 4456448 | tf_op jit(solution)/shard_map/all_gather | solution.py:37
  214.9 6.0 %copy-start.5 = (bf16[16,16]{1,0:T(8,128)(2,1)S(1)}, bf16[16,16]{1,0:T(8,128)(2,1)}, u32[]{:S(2)}) copy-start(bf16[16,16]{1,0:T(8,128)(2,1)} %param.11) | copy-start | bytes 1540
  225.8 127.0 %copy-start.3 = (f32[2048]{0:T(1024)S(1)}, f32[2048]{0:T(1024)}, u32[]{:S(2)}) copy-start(f32[2048]{0:T(1024)} %param.8) | copy-start | bytes 24580
  230.1 122.7 %all-to-all-start.1 = ((bf16[16,64,2048]{2,1,0:T(8,128)(2,1)}), bf16[16,64,2048]{2,1,0:T(8,128)(2,1)}, u32[]{:S(2)}, u32[]{:S(2)}) async-start(bf16[16,64,2048]{2,1,0:T(8,128)(2,1)} %copy.19), calls=%async_computation.1 | async-start | bytes 8388608 | tf_op jit(solution)/shard_map/all_to_all | solution.py:32
  235.0 124.7 %copy-start.4 = (f32[2048]{0:T(1024)S(1)}, f32[2048]{0:T(1024)}, u32[]{:S(2)}) copy-start(f32[2048]{0:T(1024)} %param.9) | copy-start | bytes 24580
  235.0 127.7 %all-gather.5.cloned.1.call-start = ((), (), s32[]{:S(2)}) async-start(), calls=%async_computation.3 | async-start | bytes 4456448 | tf_op jit(solution)/shard_map/all_gather | solution.py:45
  357.8 1.9 copy-start.2
  377.1 17.6 %copy-start.1 = (bf16[1024,1024]{1,0:T(8,128)(2,1)S(1)}, bf16[1024,1024]{1,0:T(8,128)(2,1)}, u32[]{:S(2)}) copy-start(bf16[1024,1024]{1,0:T(8,128)(2,1)} %param.10) | copy-start | bytes 6291460
Sparse Core Ops, SparseCore 0:
  87.8 94.8 all-gather.2
  238.0 94.8 all-gather.4
where the time goes:
time: 403 us; the launch traced here: 402 us
  waiting for transfers between devices  235 us (58%)
  local copies, waits for them, and re-layouts  66.5 us (17%)
  other arithmetic  46.3 us (11%)
  matrix products  28.3 us (7%)
  between operations  13.5 us (3%)
  starting transfers between devices  11.9 us (3%)
    all_to_all x1, waiting for transfers between devices, shards(): lax.all_to_all(within, 'seq', split_axis=1, concat_axis=0, tiled=True)  117 us
    all_to_all x1, waiting for transfers between devices, shards(): lax.all_to_all(mixed_cols, 'seq', split_axis=0, concat_axis=1, tiled=True)  117 us
    unnamed x16, local copies, waits for them, and re-layouts  32.2 us
    unnamed x1, other arithmetic  26.7 us
    convert_element_type x1, local copies, waits for them, and re-layouts, shards(): within = jnp.einsum('hp,ops->ohs', block_mix, normed.reshape(nblocks, BLK...  20.6 us
    dot_general x1, matrix products, shards(): jnp.einsum('rcf,cfd->rcd', hidden, weight_out.reshape(NCB, hidden.shape[2...  14.3 us
    reshape x1, local copies, waits for them, and re-layouts, shards(): output.reshape(rows, width)  9.34 us
    dot_general x1, matrix products, shards(): jnp.einsum('hp,ops->ohs', block_mix, normed.reshape(nblocks, BLK, width),...  9.21 us
  transfers between devices with their start and end apart: 4, of which 2 were waited for; matrix products, arithmetic and copies ran while one was open for 9% of the time, Pallas kernels for 0%

commit v1 on v0

--- a/solution.py
+++ b/solution.py
@@ -26,7 +26,10 @@
     mixed_cols = jnp.einsum(
         "ai,ijd->ajd",
         cross_mix,
-        lax.all_to_all(within, "seq", split_axis=1, concat_axis=0, tiled=True),
+        jnp.concatenate(
+            lax.all_to_all(jnp.stack(jnp.split(within, lax.axis_size("seq"), axis=1)), "seq", 0, 0),
+            axis=0,
+        ),
         preferred_element_type=jnp.float32,
     ).astype(jnp.bfloat16)
     across = lax.all_to_all(mixed_cols, "seq", split_axis=0, concat_axis=1, tiled=True)

time: 403 us -> 335 us (0.83)
  local copies, waits for them, and re-layouts: 66.5 us -> 27.8 us
  other arithmetic: 46.3 us -> 19.7 us
    unnamed x1 -> x0, other arithmetic: 26.7 us -> none
    convert_element_type x2 -> x1, local copies, waits for them, and re-layouts: 24.9 us -> 4.32 us  [shards(): mixed_cols = jnp.einsum('ai,ijd->ajd', cross_mix, jnp.concatenate(lax.all...]
    unnamed x16 -> x29, local copies, waits for them, and re-layouts: 32.2 us -> 13.6 us
    dot_general x1, matrix products: 9.21 us -> 4.96 us  [shards(): jnp.einsum('hp,ops->ohs', block_mix, normed.reshape(nblocks, BLK, width),...]
  transfers between devices with their start and end apart: 4 -> 4, of which waited for: 2 -> 2; matrix products, arithmetic and copies ran while one was open for 9% -> 6% of each run, Pallas kernels for 0% -> 0%
where the time goes in v1:
time: 335 us; the launch traced here: 334 us
  waiting for transfers between devices  235 us (70%)
  local copies, waits for them, and re-layouts  27.8 us (8%)
  matrix products  26.2 us (8%)
  other arithmetic  19.7 us (6%)
  between operations  13.5 us (4%)
  starting transfers between devices  11.9 us (4%)
    all_to_all x1, waiting for transfers between devices, shards(): lax.all_to_all(jnp.stack(jnp.split(within, lax.axis_size('seq'), axis=1))...  117 us
    all_to_all x1, waiting for transfers between devices, shards(): lax.all_to_all(mixed_cols, 'seq', split_axis=0, concat_axis=1, tiled=True)  117 us
    dot_general x1, matrix products, shards(): jnp.einsum('rcf,cfd->rcd', hidden, weight_out.reshape(NCB, hidden.shape[2...  14.3 us
    unnamed x29, local copies, waits for them, and re-layouts  13.6 us
    reshape x1, local copies, waits for them, and re-layouts, shards(): output.reshape(rows, width)  9.2 us
    convert_element_type x1, other arithmetic, shards(): (gated.astype(jnp.float32) + output.reshape(rows, width)).astype(jnp.bflo...  8.44 us
    reduce_sum x2, other arithmetic, rms_scale(): mean_square = jnp.mean(values * values, axis=-1, keepdims=True)  8.22 us
    dot_general x1, matrix products, shards(): jnp.einsum('ai,ijd->ajd', cross_mix, jnp.concatenate(lax.all_to_all(jnp.s...  6.92 us
  transfers between devices with their start and end apart: 4, of which 2 were waited for; matrix products, arithmetic and copies ran while one was open for 6% of the time, Pallas kernels for 0%

profile of v1, /device:TPU:13, one launch (start us, length us, event | category | flops | bytes accessed | tf_op | source)
XLA Modules:
  0.0 334.3 jit_solution(3114427640795503997)
XLA Ops:
  6.5 3.2 fusion.8
  9.8 0.8 copy-done.3
  10.6 5.0 %convert_bitcast_fusion.1 = bf16[1,1024,2048]{2,1,0:T(8,128)(2,1)S(1)} fusion(bf16[1024,1024]{1,0:T(8,128)(2,1)S(1)} %copy-done, bf16[1024,2048]{1,0:T(8,128)(2,1)S(1)} %copy-done.3, f32[2048]{0:T(1024)S(1)} %copy-done.4, f32[1024]{0:T(1024)S(1)} %add_rsqrt_fusion.1), kind=kOutput, calls=%fused_computation.29 | convolution fusion | flops 4305453056 | bytes 10498048 | tf_op jit(solution)/shard_map/hp,ops->ohs/dot_general | solution.py:20
  15.6 0.7 fusion.45
  16.3 0.7 fusion.44
  17.1 0.7 fusion.43
  17.8 0.7 fusion.42
  18.5 0.7 fusion.41
  19.2 0.7 fusion.40
  19.9 0.7 fusion.39
  25.7 0.7 fusion.31
  26.4 0.7 fusion.30
  27.2 6.7 %all-to-all-start = ((bf16[16,1,64,2048]{3,2,1,0:T(8,128)(2,1)}), bf16[16,1,64,2048]{3,2,1,0:T(8,128)(2,1)}, u32[]{:S(2)}, u32[]{:S(2)}) async-start(bf16[16,1,64,2048]{3,2,1,0:T(8,128)(2,1)} %fusion.30), calls=%async_computation | async-start | bytes 8388608 | tf_op jit(solution)/shard_map/all_to_all | solution.py:30
  34.6 117.0 %all-to-all-done = bf16[16,1,64,2048]{3,2,1,0:T(8,128)(2,1)} async-done(((bf16[16,1,64,2048]{3,2,1,0:T(8,128)(2,1)}), bf16[16,1,64,2048]{3,2,1,0:T(8,128)(2,1)}, u32[]{:S(2)}, u32[]{:S(2)}) %all-to-all-start) | async-done | bytes 4194336 | tf_op jit(solution)/shard_map/all_to_all | solution.py:30
  151.6 6.9 %convert_bitcast_fusion = bf16[16,64,2048]{2,0,1:T(8,128)(2,1)S(1)} fusion(bf16[16,64,2048]{2,1,0:T(8,128)(2,1)} %bitcast.19, bf16[16,16]{1,0:T(8,128)(2,1)S(1)} %copy-done.6), kind=kOutput, calls=%fused_computation.28 | convolution fusion | flops 69206016 | bytes 8389120 | tf_op jit(solution)/shard_map/ai,ijd->ajd/dot_general | solution.py:26
  158.5 4.3 %copy.17 = bf16[16,64,2048]{2,1,0:T(8,128)(2,1)} copy(bf16[16,64,2048]{2,0,1:T(8,128)(2,1)S(1)} %convert_bitcast_fusion) | data formatting | bytes 8388608 | tf_op jit(solution)/shard_map/convert_element_type | solution.py:34
  162.8 4.9 %all-to-all-start.1 = ((bf16[16,64,2048]{2,1,0:T(8,128)(2,1)}), bf16[16,64,2048]{2,1,0:T(8,128)(2,1)}, u32[]{:S(2)}, u32[]{:S(2)}) async-start(bf16[16,64,2048]{2,1,0:T(8,128)(2,1)} %copy.17), calls=%async_computation.1 | async-start | bytes 8388608 | tf_op jit(solution)/shard_map/all_to_all | solution.py:35
  168.5 117.0 %all-to-all-done.1 = bf16[16,64,2048]{2,1,0:T(8,128)(2,1)} async-done(((bf16[16,64,2048]{2,1,0:T(8,128)(2,1)}), bf16[16,64,2048]{2,1,0:T(8,128)(2,1)}, u32[]{:S(2)}, u32[]{:S(2)}) %all-to-all-start.1) | async-done | bytes 4194336 | tf_op jit(solution)/shard_map/all_to_all | solution.py:35
  285.5 5.0 %fusion.12 = (f32[1024]{0:T(1024)S(1)}, bf16[1024,2048]{1,0:T(8,128)(2,1)S(1)}) fusion(bf16[16,64,2048]{2,1,0:T(8,128)(2,1)} %all-to-all-done.1, f32[2048]{0:T(1024)S(1)} %copy-done.4, f32[1024]{0:T(1024)S(1)} %add_rsqrt_fusion.1, bf16[1024,2048]{1,0:T(8,128)(2,1)} %param.7), kind=kLoop, calls=%fused_computation.19 | loop fusion | flops 25164800 | bytes 12599296 | tf_op jit(solution)/shard_map/reduce_sum | solution.py:11
  290.5 1.9 copy-done.2
  292.4 3.0 fusion.14
  295.5 14.3 %fusion.28 = f32[4,1024,512]{1,2,0:T(8,128)} fusion(bf16[4,1024,512]{2,1,0:T(8,128)(2,1)} %bitcast.99, bf16[4,512,1024]{2,1,0:T(8,128)(2,1)} %bitcast.98, bf16[128,4,8,512]{3,2,1,0:T(8,128)(2,1)} %bitcast.97), kind=kOutput, calls=%fused_computation.32 | convolution fusion | flops 8627683328 | bytes 20971520 | tf_op jit(solution)/shard_map/rcf,cfd->rcd/dot_general | solution.py:49
  309.8 9.2 %copy.20 = f32[1024,2048]{1,0:T(8,128)} copy(f32[1024,2048]{0,1:T(8,128)} %bitcast.96) | data formatting | bytes 16777216 | tf_op jit(solution)/shard_map/reshape | solution.py:55
  319.0 8.4 %fusion.15 = bf16[1024,2048]{1,0:T(8,128)(2,1)} fusion(f32[1024,2048]{1,0:T(8,128)} %copy.20, bf16[1024,2048]{1,0:T(8,128)(2,1)} %copy-done.2), kind=kLoop, calls=%fused_computation.22 | loop fusion | flops 6291456 | bytes 16777216 | tf_op jit(solution)/shard_map/convert_element_type | solution.py:55
  (27 shorter events, 6.5 us)
Async XLA Ops:
  6.5 3.2 copy-start
  6.5 3.3 copy-start.4
  6.5 4.1 %copy-start.3 = (bf16[1024,2048]{1,0:T(8,128)(2,1)S(1)}, bf16[1024,2048]{1,0:T(8,128)(2,1)}, u32[]{:S(2)}) copy-start(bf16[1024,2048]{1,0:T(8,128)(2,1)} %param.7) | copy-start | bytes 12582916
  27.2 124.4 %copy-start.6 = (bf16[16,16]{1,0:T(8,128)(2,1)S(1)}, bf16[16,16]{1,0:T(8,128)(2,1)}, u32[]{:S(2)}) copy-start(bf16[16,16]{1,0:T(8,128)(2,1)} %param.11) | copy-start | bytes 1540
  27.2 124.4 %all-to-all-start = ((bf16[16,1,64,2048]{3,2,1,0:T(8,128)(2,1)}), bf16[16,1,64,2048]{3,2,1,0:T(8,128)(2,1)}, u32[]{:S(2)}, u32[]{:S(2)}) async-start(bf16[16,1,64,2048]{3,2,1,0:T(8,128)(2,1)} %fusion.30), calls=%async_computation | async-start | bytes 8388608 | tf_op jit(solution)/shard_map/all_to_all | solution.py:30
  33.8 261.6 %all-gather.3.cloned.1.call-start = ((), (), s32[]{:S(2)}) async-start(), calls=%async_computation.2 | async-start | bytes 4456448 | tf_op jit(solution)/shard_map/all_gather | solution.py:40
  162.8 122.7 %all-to-all-start.1 = ((bf16[16,64,2048]{2,1,0:T(8,128)(2,1)}), bf16[16,64,2048]{2,1,0:T(8,128)(2,1)}, u32[]{:S(2)}, u32[]{:S(2)}) async-start(bf16[16,64,2048]{2,1,0:T(8,128)(2,1)} %copy.17), calls=%async_computation.1 | async-start | bytes 8388608 | tf_op jit(solution)/shard_map/all_to_all | solution.py:35
  167.7 127.7 %all-gather.5.cloned.1.call-start = ((), (), s32[]{:S(2)}) async-start(), calls=%async_computation.3 | async-start | bytes 4456448 | tf_op jit(solution)/shard_map/all_gather | solution.py:48
  168.5 124.0 %copy-start.5 = (f32[2048]{0:T(1024)S(1)}, f32[2048]{0:T(1024)}, u32[]{:S(2)}) copy-start(f32[2048]{0:T(1024)} %param.9) | copy-start | bytes 24580
  290.5 1.9 copy-start.2
  319.0 8.4 %copy-start.1 = (bf16[1024,1024]{1,0:T(8,128)(2,1)S(1)}, bf16[1024,1024]{1,0:T(8,128)(2,1)}, u32[]{:S(2)}) copy-start(bf16[1024,1024]{1,0:T(8,128)(2,1)} %param.10) | copy-start | bytes 6291460
Sparse Core Ops, SparseCore 0:
  36.8 94.8 all-gather.2
  170.7 94.8 all-gather.4
